TPU v7x, 512 devices: a whole 4x4x16 slice. The times are simulated.
512 devices in a mesh: occ: 32 (over z, x_lo), aux: 16 (over x_hi, y, core).
Axes of the slice: x: 4 (x_hi: 2, x_lo: 2; x = x_hi * 2 + x_lo), y: 4, z: 16, core: 2. Of those that a mesh axis runs over, the one named last changes fastest.
Arguments:
- orbital_factors: bfloat16 [64, 256, 20480], P('occ', None, 'aux'), may hold values from -0.41992188 to 0.41992188
- occ_energy: bfloat16 [64], P('occ'), may hold values from -2 to -0.5
- vir_energy: float32 [256], replicated, may hold values from 0.5 to 3
- pair_kept: int32 [32, 2], P('occ'), may hold values 0 or 1
Outputs:
- gamma: float32 [64, 256, 20480], P('occ', None, 'aux')
All inputs are finite; a program needn't handle non-finite values. No bound on the sum of `pair_kept` on one device may be relied on, other than what follows from the above.
Results may differ from a plain program's by a relative error of at most 0.0034.
Values may be sent and summed in bfloat16 or wider, within the bound.
A program may use at most 64 MiB of HBM per device.

v0:
```python
import jax
import jax.numpy as jnp
from jax import lax
from jax.sharding import PartitionSpec as P


def from_behind(x, axis, by):
    devices = lax.axis_size(axis)
    return lax.ppermute(x, axis, [(i, (i + by) % devices) for i in range(devices)])


def on_device(orbital_factors, occ_energy, vir_energy, pair_kept):
    occ_dev, slab, aux_dev = orbital_factors.shape
    width = occ_dev * slab
    own_rows = orbital_factors.reshape(width, aux_dev)
    own_e = occ_energy.astype(jnp.float32)
    gamma = jnp.zeros((width, aux_dev), jnp.float32)
    for offset_step in range(pair_kept.shape[1]):
        partner_factors, partner_energy = from_behind(
            (orbital_factors, occ_energy), "occ", -(offset_step + 1)
        )
        partner_rows = partner_factors.reshape(width, aux_dev)
        partner_e = partner_energy.astype(jnp.float32)
        flag = pair_kept[0, offset_step].astype(jnp.float32)
        product = jnp.dot(own_rows, partner_rows.T, preferred_element_type=jnp.float32)
        blocks = product.reshape(occ_dev, slab, occ_dev, slab)
        mixed = 2.0 * blocks - jnp.transpose(blocks, (0, 3, 2, 1))
        total = lax.psum(mixed, "aux")
        denom = (
            own_e[:, None, None, None]
            + partner_e[None, None, :, None]
            - vir_energy[None, :, None, None]
            - vir_energy[None, None, None, :]
        )
        tilde = (flag * total / denom).astype(jnp.bfloat16)
        tilde_rows = tilde.reshape(width, width)
        own_term = jnp.dot(tilde_rows, partner_rows, preferred_element_type=jnp.float32)
        back_term = lax.dot_general(
            tilde_rows, own_rows, (((0,), (0,)), ((), ())), preferred_element_type=jnp.float32
        )
        own_term, back_term = (own_term, back_term)
        returned = from_behind(back_term.astype(jnp.bfloat16), "occ", offset_step + 1)
        gamma = gamma + own_term + returned.astype(jnp.float32)
    return gamma.reshape(occ_dev, slab, aux_dev)


def solution(mesh):
    in_specs = (P("occ", None, "aux"), P("occ"), P(), P("occ", None))
    out_specs = P("occ", None, "aux")
    return jax.shard_map(
        on_device, mesh=mesh, in_specs=in_specs, out_specs=out_specs, check_vma=False
    )
```

profile of v0, /device:TPU:2, one launch (start us, length us, event | category | flops | bytes accessed | tf_op | source)
XLA Modules:
  0.0 313.0 jit_solution(9923133824051672020)
XLA Ops:
  6.5 0.0 all-reduce.3.cloned.1.call-start
  6.5 7.8 %collective-permute-start = (bf16[2,256,1280]{2,1,0:T(8,128)(2,1)}, bf16[2,256,1280]{2,1,0:T(8,128)(2,1)S(1)}, u32[]{:S(2)}, u32[]{:S(2)}) collective-permute-start(bf16[2,256,1280]{2,1,0:T(8,128)(2,1)} %param.4), channel_id=1, source_target_pairs={{0,496},{16,0},{32,16},{48,32},{64,48},{80,64},{96,80},{112,96},{1... | collective-permute-start | bytes 3932168 | tf_op jit(solution)/shard_map/ppermute | solution.py:9
  14.4 6.0 %collective-permute-start.3 = (bf16[2,256,1280]{2,1,0:T(8,128)(2,1)}, bf16[2,256,1280]{2,1,0:T(8,128)(2,1)}, u32[]{:S(2)}, u32[]{:S(2)}) collective-permute-start(bf16[2,256,1280]{2,1,0:T(8,128)(2,1)} %param.4), channel_id=1, source_target_pairs={{0,480},{16,496},{32,0},{48,16},{64,32},{80,48},{96,64},{112,80},{... | collective-permute-start | bytes 3932168 | tf_op jit(solution)/shard_map/ppermute | solution.py:9
  20.4 20.8 %collective-permute-done = bf16[2,256,1280]{2,1,0:T(8,128)(2,1)S(1)} collective-permute-done((bf16[2,256,1280]{2,1,0:T(8,128)(2,1)}, bf16[2,256,1280]{2,1,0:T(8,128)(2,1)S(1)}, u32[]{:S(2)}, u32[]{:S(2)}) %collective-permute-start) | collective-permute-done | bytes 1310752 | tf_op jit(solution)/shard_map/ppermute | solution.py:9
  41.2 2.2 fusion.5
  43.4 0.3 copy.7
  43.7 0.0 copy-start.2
  43.7 1.1 bitcast_subtract_fusion.1
  44.8 3.6 %collective-permute-done.3 = bf16[2,256,1280]{2,1,0:T(8,128)(2,1)} collective-permute-done((bf16[2,256,1280]{2,1,0:T(8,128)(2,1)}, bf16[2,256,1280]{2,1,0:T(8,128)(2,1)}, u32[]{:S(2)}, u32[]{:S(2)}) %collective-permute-start.3) | collective-permute-done | bytes 1310752 | tf_op jit(solution)/shard_map/ppermute | solution.py:9
  48.4 0.0 copy-done.2
  48.4 2.2 fusion.2
  50.6 0.3 copy.9
  51.0 1.1 bitcast_subtract_fusion
  52.1 0.0 copy-start.4
  52.1 0.0 copy-start.1
  52.1 0.0 copy-start
  52.1 0.0 all-reduce.3.cloned.1.call-update
  52.1 0.6 copy-done.4
  52.7 9.6 %collective-permute-start.4 = (bf16[2]{0:T(256)(128)(2,1)S(1)}, bf16[2]{0:T(256)(128)(2,1)S(1)}, u32[]{:S(2)}, u32[]{:S(2)}) collective-permute-start(bf16[2]{0:T(256)(128)(2,1)S(1)} %copy-done.4), channel_id=1, source_target_pairs={{0,480},{16,496},{32,0},{48,16},{64,32},{80,48},{96,64},{112,80},{... | collective-permute-start | bytes 20 | tf_op jit(solution)/shard_map/ppermute | solution.py:9
  62.3 25.3 %collective-permute-start.1 = (bf16[2]{0:T(256)(128)(2,1)S(1)}, bf16[2]{0:T(256)(128)(2,1)S(1)}, u32[]{:S(2)}, u32[]{:S(2)}) collective-permute-start(bf16[2]{0:T(256)(128)(2,1)S(1)} %copy-done.4), channel_id=1, source_target_pairs={{0,496},{16,0},{32,16},{48,32},{64,48},{80,64},{96,80},{112,96},{1... | collective-permute-start | bytes 20 | tf_op jit(solution)/shard_map/ppermute | solution.py:9
  87.6 0.0 copy-done.1
  87.6 0.6 fusion.8
  89.4 0.0 collective-permute-done.4
  89.4 0.0 collective-permute-done.1
  89.5 0.1 broadcast_add_fusion.1
  89.5 0.0 copy-done
  89.5 0.1 broadcast_subtract_fusion.1
  89.6 145.6 %all-reduce.3.cloned.1.call-done = (f32[2,256,2,256]{1,3,2,0:T(8,128)}, f32[2,256,2,256]{1,3,2,0:T(8,128)}) async-done(((f32[2,256,2,256]{1,3,2,0:T(8,128)}, f32[2,256,2,256]{1,3,2,0:T(8,128)}), (f32[2,256,2,256]{1,3,2,0:T(8,128)}, f32[2,256,2,256]{1,3,2,0:T(8,128)})) %all-reduce.3.cloned.1.call-update) | async-done | bytes 2097168 | tf_op jit(solution)/shard_map/psum | solution.py:28
  235.2 1.9 divide_convert_fusion.1
  237.1 0.5 copy.8
  237.6 0.1 copy.12
  237.7 0.5 copy.10
  238.1 0.1 copy.13
  238.2 0.0 copy-start.3
  238.2 2.3 convolution_convert_fusion
  240.5 0.0 copy-done.3
  240.5 0.9 convolution_convert_fusion.1
  241.4 4.1 %collective-permute-start.2 = (bf16[512,1280]{1,0:T(8,128)(2,1)S(1)}, bf16[512,1280]{1,0:T(8,128)(2,1)S(1)}, u32[]{:S(2)}, u32[]{:S(2)}) collective-permute-start(bf16[512,1280]{1,0:T(8,128)(2,1)S(1)} %convolution_convert_fusion.1), channel_id=1, source_target_pairs={{0,16},{16,32},{32,48},{48,64},{64,80},{80,96},{96,112},{112,128},... | collective-permute-start | bytes 3932168 | tf_op jit(solution)/shard_map/ppermute | solution.py:9
  245.6 3.5 %collective-permute-start.5 = (bf16[512,1280]{1,0:T(8,128)(2,1)S(1)}, bf16[512,1280]{1,0:T(8,128)(2,1)S(1)}, u32[]{:S(2)}, u32[]{:S(2)}) collective-permute-start(bf16[512,1280]{1,0:T(8,128)(2,1)S(1)} %convolution_convert_fusion), channel_id=1, source_target_pairs={{0,32},{16,48},{32,64},{48,80},{64,96},{80,112},{96,128},{112,144}... | collective-permute-start | bytes 3932168 | tf_op jit(solution)/shard_map/ppermute | solution.py:9
  249.0 2.2 fusion.9
  251.2 23.6 %collective-permute-done.2 = bf16[512,1280]{1,0:T(8,128)(2,1)S(1)} collective-permute-done((bf16[512,1280]{1,0:T(8,128)(2,1)S(1)}, bf16[512,1280]{1,0:T(8,128)(2,1)S(1)}, u32[]{:S(2)}, u32[]{:S(2)}) %collective-permute-start.2) | collective-permute-done | bytes 1310752 | tf_op jit(solution)/shard_map/ppermute | solution.py:9
  274.8 28.9 %collective-permute-done.5 = bf16[512,1280]{1,0:T(8,128)(2,1)S(1)} collective-permute-done((bf16[512,1280]{1,0:T(8,128)(2,1)S(1)}, bf16[512,1280]{1,0:T(8,128)(2,1)S(1)}, u32[]{:S(2)}, u32[]{:S(2)}) %collective-permute-start.5) | collective-permute-done | bytes 1310752 | tf_op jit(solution)/shard_map/ppermute | solution.py:9
  303.6 2.5 fusion.1
  (3 shorter events, 0.0 us)
Async XLA Ops:
  6.5 228.7 %all-reduce.3.cloned.1.call-start = ((), (), s32[]{:S(2)}) async-start(), calls=%async_computation | async-start | bytes 4194304 | tf_op jit(solution)/shard_map/psum | solution.py:28
  6.5 34.7 %collective-permute-start = (bf16[2,256,1280]{2,1,0:T(8,128)(2,1)}, bf16[2,256,1280]{2,1,0:T(8,128)(2,1)S(1)}, u32[]{:S(2)}, u32[]{:S(2)}) collective-permute-start(bf16[2,256,1280]{2,1,0:T(8,128)(2,1)} %param.4), channel_id=1, source_target_pairs={{0,496},{16,0},{32,16},{48,32},{64,48},{80,64},{96,80},{112,96},{1... | collective-permute-start | bytes 3932168 | tf_op jit(solution)/shard_map/ppermute | solution.py:9
  14.4 34.1 %collective-permute-start.3 = (bf16[2,256,1280]{2,1,0:T(8,128)(2,1)}, bf16[2,256,1280]{2,1,0:T(8,128)(2,1)}, u32[]{:S(2)}, u32[]{:S(2)}) collective-permute-start(bf16[2,256,1280]{2,1,0:T(8,128)(2,1)} %param.4), channel_id=1, source_target_pairs={{0,480},{16,496},{32,0},{48,16},{64,32},{80,48},{96,64},{112,80},{... | collective-permute-start | bytes 3932168 | tf_op jit(solution)/shard_map/ppermute | solution.py:9
  43.7 4.7 %copy-start.2 = (bf16[2,256,1280]{2,1,0:T(8,128)(2,1)S(1)}, bf16[2,256,1280]{2,1,0:T(8,128)(2,1)}, u32[]{:S(2)}) copy-start(bf16[2,256,1280]{2,1,0:T(8,128)(2,1)} %param.4) | copy-start | bytes 3932164
  52.1 0.7 copy-start.4
  52.1 35.6 %copy-start.1 = (s32[1,2]{1,0:T(1,128)S(1)}, s32[1,2]{1,0:T(1,128)}, u32[]{:S(2)}) copy-start(s32[1,2]{1,0:T(1,128)} %param.7) | copy-start | bytes 28
  52.1 37.5 %copy-start = (f32[256]{0:T(256)S(1)}, f32[256]{0:T(256)}, u32[]{:S(2)}) copy-start(f32[256]{0:T(256)} %param.6) | copy-start | bytes 3076
  52.7 36.7 %collective-permute-start.4 = (bf16[2]{0:T(256)(128)(2,1)S(1)}, bf16[2]{0:T(256)(128)(2,1)S(1)}, u32[]{:S(2)}, u32[]{:S(2)}) collective-permute-start(bf16[2]{0:T(256)(128)(2,1)S(1)} %copy-done.4), channel_id=1, source_target_pairs={{0,480},{16,496},{32,0},{48,16},{64,32},{80,48},{96,64},{112,80},{... | collective-permute-start | bytes 20 | tf_op jit(solution)/shard_map/ppermute | solution.py:9
  62.3 27.1 %collective-permute-start.1 = (bf16[2]{0:T(256)(128)(2,1)S(1)}, bf16[2]{0:T(256)(128)(2,1)S(1)}, u32[]{:S(2)}, u32[]{:S(2)}) collective-permute-start(bf16[2]{0:T(256)(128)(2,1)S(1)} %copy-done.4), channel_id=1, source_target_pairs={{0,496},{16,0},{32,16},{48,32},{64,48},{80,64},{96,80},{112,96},{1... | collective-permute-start | bytes 20 | tf_op jit(solution)/shard_map/ppermute | solution.py:9
  238.2 2.3 copy-start.3
  241.4 33.3 %collective-permute-start.2 = (bf16[512,1280]{1,0:T(8,128)(2,1)S(1)}, bf16[512,1280]{1,0:T(8,128)(2,1)S(1)}, u32[]{:S(2)}, u32[]{:S(2)}) collective-permute-start(bf16[512,1280]{1,0:T(8,128)(2,1)S(1)} %convolution_convert_fusion.1), channel_id=1, source_target_pairs={{0,16},{16,32},{32,48},{48,64},{64,80},{80,96},{96,112},{112,128},... | collective-permute-start | bytes 3932168 | tf_op jit(solution)/shard_map/ppermute | solution.py:9
  245.6 58.1 %collective-permute-start.5 = (bf16[512,1280]{1,0:T(8,128)(2,1)S(1)}, bf16[512,1280]{1,0:T(8,128)(2,1)S(1)}, u32[]{:S(2)}, u32[]{:S(2)}) collective-permute-start(bf16[512,1280]{1,0:T(8,128)(2,1)S(1)} %convolution_convert_fusion), channel_id=1, source_target_pairs={{0,32},{16,48},{32,64},{48,80},{64,96},{80,112},{96,128},{112,144}... | collective-permute-start | bytes 3932168 | tf_op jit(solution)/shard_map/ppermute | solution.py:9
Sparse Core Ops, SparseCore 0:
  52.2 182.9 all-reduce.2
where the time goes:
time: 313 us
  waiting for transfers between devices  222 us (71%)
  starting transfers between devices  56.3 us (18%)
  between operations  14.8 us (5%)
  matrix products  12.2 us (4%)
  other arithmetic  4.31 us (1%)
    psum x1, waiting for transfers between devices, on_device(): total = lax.psum(mixed, 'aux')  146 us
    ppermute x6, waiting for transfers between devices, from_behind(): lax.ppermute(x, axis, [(i, (i + by) % devices) for i in range(devices)])  76.9 us
    ppermute x6, starting transfers between devices, from_behind(): lax.ppermute(x, axis, [(i, (i + by) % devices) for i in range(devices)])  56.3 us
  transfers between devices with their start and end apart: 7, of which 5 were waited for; matrix products, arithmetic and copies ran while one was open for 2% of the time, Pallas kernels for 0%

commit v1 on v0

v1 whole, which is shorter than its diff:
```python
import functools

import jax
import jax.numpy as jnp
from jax import lax
from jax.experimental import pallas as pl
from jax.experimental.pallas import tpu as pltpu
from jax.sharding import PartitionSpec as P

F32 = jnp.float32
BF16 = jnp.bfloat16
NT = (((1,), (1,)), ((), ()))

X, F, R, D, ME = range(5)
KINDS = ((ME, X), (X, F), (ME, F), (R, ME))
PAIRS = ((ME, X), (ME, F), (R, ME), (D, ME))


def kernel(
    planes, b_hbm, small_ref, out_hbm,
    bb, small, k, rc, ry, rx, cx, cr, cf, t, tt, g,
    send, recv, local, out_sem,
):
    slab = k.shape[1]
    rows = slab // 16
    half = b_hbm.shape[1] // 2

    occ, aux = lax.axis_index("occ"), lax.axis_index("aux")
    z, lo = occ // 2, lax.rem(occ, 2)
    core, y, xh = lax.rem(aux, 2), lax.rem(aux // 2, 4), aux // 8
    ahead = lax.rem(z + planes + 1 - 2 * lo, planes)
    behind = lax.rem(z + planes - 1 + 2 * lo, planes)
    occ_of = (z * 2 + 1 - lo, ahead * 2 + lo, behind * 2 + lo, behind * 2 + 1 - lo)

    def aux_of(xh_, y_, core_):
        return (xh_ * 4 + y_) * 2 + core_

    y1, y2, y3 = y + 1 - 2 * lax.rem(y, 2), lax.rem(y + 2, 4), 3 - y
    other_core, other_xh = 1 - core, 1 - xh
    to_core = (occ, aux_of(xh, y, other_core))
    to_y1 = (occ, aux_of(xh, y1, core))
    to_y3 = (occ, aux_of(xh, y3, core))
    to_xh = (occ, aux_of(other_xh, y, core))
    to = [(o, aux) for o in occ_of]

    def device(where):
        return {"occ": where[0], "aux": where[1]}

    def copy(n, src, dst, where):
        return pltpu.make_async_remote_copy(
            src_ref=src, dst_ref=dst, send_sem=send.at[n], recv_sem=recv.at[n],
            device_id=device(where), device_id_type=pl.DeviceIdType.MESH,
        )

    own = pltpu.make_async_copy(b_hbm, bb.at[ME], local.at[0])
    own.start()
    barrier = pltpu.get_barrier_semaphore()
    for where in (*to, to_core, to_y1, to_y3, to_xh):
        pl.semaphore_signal(barrier, inc=1, device_id=device(where), device_id_type=pl.DeviceIdType.MESH)
    pl.semaphore_wait(barrier, 8)

    mine = pl.ds(pl.multiple_of(half * (1 - lo), half), half)
    others = pl.ds(pl.multiple_of(half * lo, half), half)

    started = []

    def start(*args):
        c = copy(*args)
        c.start()
        started.append(c)
        return c

    first_x = start(0, b_hbm.at[:, others], bb.at[X, :, others], to[X])
    first_f = start(1, b_hbm.at[:, mine], bb.at[F, :, mine], to[R])
    first_r = start(2, b_hbm.at[:, others], bb.at[R, :, others], to[F])
    smalls = [
        start(8 + slot, small_ref.at[pl.ds(rows, 8)], small.at[slot], to[back])
        for slot, back in ((X, X), (F, R), (R, F), (D, D))
    ]

    def pair_sums(kind, columns):
        p, q = KINDS[kind]
        first, second = p + lo * (q - p), q + lo * (p - q)

        def block(i, j):
            a = bb[first, i * slab:(i + 1) * slab, columns]
            b = bb[second, j * slab:(j + 1) * slab, columns]
            direct = lax.dot_general(a + a, b, NT, preferred_element_type=F32)
            exchanged = lax.dot_general(b, a, NT, preferred_element_type=F32)
            k[2 * kind + i, :, j * slab:(j + 1) * slab] = direct - exchanged

        for i in range(2):
            for j in range(2):
                block(i, j)

    own.wait()
    first_x.wait_recv()
    pair_sums(0, mine)
    first_f.wait_recv()
    second = [
        start(3, bb.at[X, :, mine], bb.at[D, :, mine], to[F]),
        start(4, bb.at[F, :, mine], bb.at[D, :, mine], to[X]),
    ]
    first_r.wait_recv()
    second += [
        start(5, b_hbm.at[:, mine], bb.at[X, :, mine], to[X]),
        start(6, b_hbm.at[:, others], bb.at[F, :, others], to[R]),
        start(7, b_hbm.at[:, mine], bb.at[R, :, mine], to[F]),
    ]
    pair_sums(1, mine)
    pair_sums(2, mine)
    pair_sums(3, others)

    def rows_of(core_, y_, xh_):
        c = core_ * 8 + y_ * 2 + xh_
        return pl.ds(pl.multiple_of(c * rows, rows), rows)

    def part(core_, y_, xh_):
        return k.at[:, rows_of(core_, y_, xh_)]

    def add(core_, y_, xh_, got):
        r = rows_of(core_, y_, xh_)
        k[:, r, :] = k[:, r, :] + got[...]

    n = 12
    stage = []
    for y_ in range(4):
        for x_ in range(2):
            stage.append((start(n, part(other_core, y_, x_), rc.at[y_ * 2 + x_], to_core), y_, x_))
            n += 1
    for c, y_, x_ in stage:
        c.wait_recv()
        add(core, y_, x_, rc.at[y_ * 2 + x_])

    one = [
        start(20, part(core, y2, 0), ry.at[0], to_y1),
        start(21, part(core, y2, 1), ry.at[1], to_y3),
        start(22, part(core, y1, 0), ry.at[2], to_y1),
        start(23, part(core, y3, 1), ry.at[3], to_y3),
    ]
    one[0].wait_recv()
    add(core, y3, 0, ry.at[0])
    two = [start(24, part(core, y3, 0), ry.at[4], to_y3)]
    one[1].wait_recv()
    add(core, y1, 1, ry.at[1])
    two.append(start(25, part(core, y1, 1), ry.at[5], to_y1))
    one[2].wait_recv()
    add(core, y, 0, ry.at[2])
    one[3].wait_recv()
    add(core, y, 1, ry.at[3])
    two[0].wait_recv()
    add(core, y, 0, ry.at[4])
    two[1].wait_recv()
    add(core, y, 1, ry.at[5])
    across = start(26, part(core, y, other_xh), rx, to_xh)
    across.wait_recv()
    add(core, y, xh, rx)

    mine_r = rows_of(core, y, xh)
    from_x = start(27, k.at[0:4, mine_r], cx, to[X])
    from_r = start(28, k.at[2:6, mine_r], cr, to[F])
    from_f = start(29, k.at[6:8, mine_r], cf, to[R])
    for c in smalls:
        c.wait_recv()
    small[ME] = small_ref[rows:rows + 8]
    from_x.wait_recv()
    from_r.wait_recv()
    from_f.wait_recv()
    totals = (
        lambda i: k[i, mine_r, :] + cx[i],
        lambda i: k[4 + i, mine_r, :] + cf[i],
        lambda i: k[6 + i, mine_r, :] + cr[2 + i],
        lambda i: cx[2 + i] + cr[i],
    )
    virtual = small_ref[0:rows]
    for pair, (p, q) in enumerate(PAIRS):
        first, second_ = p + lo * (q - p), q + lo * (p - q)
        flag_row = 2 + (0 if pair in (X, D) else 1)
        flag = small[first, flag_row:flag_row + 1]
        for i in range(2):
            total = totals[pair](i)
            for j in range(2):
                at = slice(j * slab, (j + 1) * slab)
                energy = small[first, i:i + 1] + small[second_, j:j + 1]
                t[2 * pair + i, mine_r, at] = (flag * total[:, at] / (energy - virtual)).astype(BF16)

    def rows_t(core_, y_, xh_):
        return t.at[:, rows_of(core_, y_, xh_)]

    def spread(n, core_, y_, xh_, where):
        return start(n, rows_t(core_, y_, xh_), rows_t(core_, y_, xh_), where)

    base = 30
    got = [spread(base, core, y, xh, to_xh)]
    a0 = spread(base + 1, core, y, xh, to_y3)
    b0 = spread(base + 2, core, y, xh, to_y1)
    s0 = spread(base + 3, core, y, xh, to_core)
    got[0].wait_recv()
    s1 = spread(base + 4, core, y, other_xh, to_core)
    a1 = spread(base + 5, core, y, other_xh, to_y3)
    b1 = spread(base + 6, core, y, other_xh, to_y1)
    a0.wait_recv()
    a2 = spread(base + 7, core, y3, xh, to_y1)
    s2 = spread(base + 8, core, y3, xh, to_core)
    b0.wait_recv()
    s3 = spread(base + 9, core, y1, xh, to_core)
    a1.wait_recv()
    s4 = spread(base + 10, core, y3, other_xh, to_core)
    b1.wait_recv()
    b2 = spread(base + 11, core, y1, other_xh, to_y3)
    s5 = spread(base + 12, core, y1, other_xh, to_core)
    a2.wait_recv()
    s6 = spread(base + 13, core, y2, xh, to_core)
    b2.wait_recv()
    s7 = spread(base + 14, core, y2, other_xh, to_core)
    for c in (s0, s1, s2, s3, s4, s5, s6, s7):
        c.wait_recv()

    turned = 2 * (1 - lo)
    straight = 2 * lo
    for u in range(2):
        for i in range(2):
            for j in range(2):
                block = t[2 * (turned + u) + i, :, j * slab:(j + 1) * slab]
                tt[2 * u + j, :, i * slab:(i + 1) * slab] = block.T

    for c in second:
        c.wait_recv()
    width = g.shape[2]
    results = []
    for s in range(2 * half // width):
        at = slice(s * width, (s + 1) * width)
        for i in range(2):
            total = jnp.zeros((slab, width), F32)
            for u in range(2):
                total += jnp.dot(t[2 * (straight + u) + i], bb[straight + u, :, at], preferred_element_type=F32)
                total += jnp.dot(tt[2 * u + i], bb[turned + u, :, at], preferred_element_type=F32)
            g[s, i * slab:(i + 1) * slab] = total
        result = pltpu.make_async_copy(g.at[s], out_hbm.at[:, at], out_sem.at[s])
        result.start()
        results.append(result)
    for c in started:
        c.wait_send()
    for c in results:
        c.wait()


def on_device(planes, orbital_factors, occ_energy, vir_energy, pair_kept):
    occ_dev, slab, aux_dev = orbital_factors.shape
    width = occ_dev * slab
    rows = slab // 16
    chunks = 5 if aux_dev % 640 == 0 else 2
    aux = lax.axis_index("aux")
    c = lax.rem(aux, 2) * 8 + lax.rem(aux // 2, 4) * 2 + aux // 8
    mine = lax.dynamic_slice_in_dim(vir_energy, c * rows, rows, 0)
    virtual = mine[:, None] + vir_energy[None, :]
    scalars = jnp.concatenate([occ_energy.astype(F32), pair_kept[0].astype(F32), jnp.zeros((4,), F32)])
    small = jnp.concatenate([virtual, jnp.broadcast_to(scalars[:, None], (8, slab))])
    copies = 45
    gamma = pl.pallas_call(
        functools.partial(kernel, planes),
        out_shape=jax.ShapeDtypeStruct((width, aux_dev), F32),
        in_specs=[pl.BlockSpec(memory_space=pl.ANY), pl.BlockSpec(memory_space=pltpu.VMEM)],
        out_specs=pl.BlockSpec(memory_space=pl.ANY),
        scratch_shapes=[
            pltpu.VMEM((5, width, aux_dev), BF16),
            pltpu.VMEM((5, 8, slab), F32),
            pltpu.VMEM((8, slab, width), F32),
            pltpu.VMEM((8, 8, rows, width), F32),
            pltpu.VMEM((6, 8, rows, width), F32),
            pltpu.VMEM((8, rows, width), F32),
            pltpu.VMEM((4, rows, width), F32),
            pltpu.VMEM((4, rows, width), F32),
            pltpu.VMEM((2, rows, width), F32),
            pltpu.VMEM((8, slab, width), BF16),
            pltpu.VMEM((4, slab, width), BF16),
            pltpu.VMEM((chunks, width, aux_dev // chunks), F32),
            pltpu.SemaphoreType.DMA((copies,)),
            pltpu.SemaphoreType.DMA((copies,)),
            pltpu.SemaphoreType.DMA((1,)),
            pltpu.SemaphoreType.DMA((chunks,)),
        ],
        compiler_params=pltpu.CompilerParams(
            collective_id=0, has_side_effects=True, vmem_limit_bytes=48 * 1024 * 1024
        ),
        cost_estimate=pl.CostEstimate(
            flops=12 * width * width * aux_dev, bytes_accessed=6 * width * aux_dev, transcendentals=0
        ),
    )(orbital_factors.reshape(width, aux_dev), small)
    return gamma.reshape(occ_dev, slab, aux_dev)


def solution(mesh):
    in_specs = (P("occ", None, "aux"), P("occ"), P(), P("occ", None))
    out_specs = P("occ", None, "aux")
    return jax.shard_map(
        functools.partial(on_device, mesh.shape["occ"] // 2),
        mesh=mesh, in_specs=in_specs, out_specs=out_specs, check_vma=False,
    )
```

time: 313 us -> 95.9 us (0.31)
  the two profiles are of different devices: /device:TPU:2 before, /device:TPU:1 now
where the time goes in v1:
time: 95.9 us; the launch traced here: 95.7 us
  Pallas kernels  89.9 us (94%)
  local copies, waits for them, and re-layouts  3.57 us (4%)
  other arithmetic  2.22 us (2%)
    pallas_call x1, Pallas kernels, on_device(): pl.pallas_call(functools.partial(kernel, planes), out_shape=jax.ShapeDtyp...  89.9 us
    unnamed x3, local copies, waits for them, and re-layouts  2.81 us

profile of v1, /device:TPU:1, one launch (start us, length us, event | category | flops | bytes accessed | tf_op | source)
XLA Modules:
  0.0 95.7 jit_solution(9610527480667906689)
XLA Ops:
  0.0 0.8 dynamic_slice.3
  0.8 0.7 convert_element_type.9
  1.4 0.7 convert_bitcast_fusion
  2.1 0.1 pad_maximum_fusion.1
  2.1 0.8 broadcast_add_fusion
  2.9 0.1 pad_maximum_fusion.small_ref
  3.0 0.0 copy-start
  3.0 1.3 %copy-done = bf16[2,256,1280]{2,1,0:T(8,128)(2,1)S(1)} copy-done((bf16[2,256,1280]{2,1,0:T(8,128)(2,1)S(1)}, bf16[2,256,1280]{2,1,0:T(8,128)(2,1)}, u32[]{:S(2)}) %copy-start) | copy-done | bytes 1310744
  4.3 89.9 %shard_map.46 = f32[512,1280]{1,0:T(8,128)S(1)} custom-call(bf16[512,1280]{1,0:T(8,128)(2,1)S(1)} %bitcast.5, f32[24,256]{1,0:T(8,128)S(1)} %pad_maximum_fusion.small_ref), custom_call_target="tpu_custom_call" | custom-call | flops 4026531840 | bytes 3932160 | tf_op jit(solution)/shard_map/pallas_call | solution.py:260
  94.2 1.5 %copy.6 = f32[2,256,1280]{2,1,0:T(8,128)} copy(f32[2,256,1280]{2,1,0:T(8,128)S(1)} %bitcast.4) | data formatting | bytes 5242880
  (1 shorter events, 0.0 us)
Async XLA Ops:
  3.0 1.3 %copy-start = (bf16[2,256,1280]{2,1,0:T(8,128)(2,1)S(1)}, bf16[2,256,1280]{2,1,0:T(8,128)(2,1)}, u32[]{:S(2)}) copy-start(bf16[2,256,1280]{2,1,0:T(8,128)(2,1)} %param.4) | copy-start | bytes 3932164

commit v2 on v0

v2 whole, which is shorter than its diff:
```python
import functools

import jax
import jax.numpy as jnp
from jax import lax
from jax.experimental import pallas as pl
from jax.experimental.pallas import tpu as pltpu
from jax.sharding import PartitionSpec as P

F32 = jnp.float32
BF16 = jnp.bfloat16
I16 = jnp.int16
TOP = 32760.0
NT = (((1,), (1,)), ((), ()))

X, F, R, D, ME = range(5)
KINDS = ((ME, X), (X, F), (ME, F), (ME, R))
KX, KXF, KF, KR = range(4)
BATCHES = (
    ((KX, 0, 0), (KX, 1, 0), (KXF, 0, 0), (KF, 0, 0), (KF, 1, 0), (KR, 0, 0), (KR, 1, 0)),
    ((KX, 0, 1), (KX, 1, 1), (KXF, 0, 1), (KXF, 1, 0), (KXF, 1, 1), (KF, 0, 1), (KF, 1, 1), (KR, 0, 1), (KR, 1, 1)),
)
BLOCKS = BATCHES[0] + BATCHES[1]
AT = {block: n for n, block in enumerate(BLOCKS)}
SPANS = ((0, 7), (7, 16))
TO_X = ((0, 3), (7, 12))
TO_F = ((2, 5), (9, 14))
TO_R = ((5, 7), (14, 16))
CUT = (3, 12)
SCALES = ((0, 8), (8, 24))


def kernel(
    planes, b_hbm, e_ref, v_ref, kept_ref, out_hbm,
    bb, small, k, rc, q, scale, ry, ry_scale, ys, rx, p, cx, cr, cf, t, tt, g,
    send, recv, local, out_sem,
):
    slab = k.shape[1]
    rows, yrows, crows = slab // 16, slab // 8, slab // 2
    half = b_hbm.shape[1] // 2

    occ, aux = lax.axis_index("occ"), lax.axis_index("aux")
    z, lo = occ // 2, lax.rem(occ, 2)
    core, y, xh = lax.rem(aux, 2), lax.rem(aux // 2, 4), aux // 8
    ahead = lax.rem(z + planes + 1 - 2 * lo, planes)
    behind = lax.rem(z + planes - 1 + 2 * lo, planes)
    occ_of = (z * 2 + 1 - lo, ahead * 2 + lo, behind * 2 + lo, behind * 2 + 1 - lo)

    def aux_of(xh_, y_, core_):
        return (xh_ * 4 + y_) * 2 + core_

    y1, y2, y3 = y + 1 - 2 * lax.rem(y, 2), lax.rem(y + 2, 4), 3 - y
    other_core, other_xh = 1 - core, 1 - xh
    to_core = (occ, aux_of(xh, y, other_core))
    to_y = [(occ, aux_of(xh, y_, core)) for y_ in (y1, y2, y3)]
    to_xh = (occ, aux_of(other_xh, y, core))
    to = [(o, aux) for o in occ_of]

    def device(where):
        return {"occ": where[0], "aux": where[1]}

    started = []
    numbers = iter(range(send.shape[0]))

    def start(src, dst, where):
        n = next(numbers)
        c = pltpu.make_async_remote_copy(
            src_ref=src, dst_ref=dst, send_sem=send.at[n], recv_sem=recv.at[n],
            device_id=device(where), device_id_type=pl.DeviceIdType.MESH,
        )
        c.start()
        started.append(c)
        return c

    own = pltpu.make_async_copy(b_hbm, bb.at[ME], local.at[0])
    own.start()
    barrier = pltpu.get_barrier_semaphore()
    for where in (*to, to_core, *to_y, to_xh):
        pl.semaphore_signal(barrier, inc=1, device_id=device(where), device_id_type=pl.DeviceIdType.MESH)

    for i in range(2):
        small[ME, i:i + 1] = jnp.broadcast_to(e_ref[:, i:i + 1].astype(F32), (1, slab))
        small[ME, 2 + i:3 + i] = jnp.broadcast_to(kept_ref[:, i:i + 1].astype(F32), (1, slab))
    small[ME, 4:8] = jnp.zeros((4, slab), F32)
    my_row = core * crows + y * yrows + xh * rows
    spot = lax.broadcasted_iota(jnp.int32, (rows, slab), 1) - lax.broadcasted_iota(jnp.int32, (rows, slab), 0)
    mine_v = jnp.sum(jnp.where(spot == my_row, v_ref[...], 0.0), axis=1, keepdims=True)
    virtual = mine_v + v_ref[...]

    pl.semaphore_wait(barrier, 9)

    mine = pl.ds(pl.multiple_of(half * (1 - lo), half), half)
    others = pl.ds(pl.multiple_of(half * lo, half), half)

    lo_mine, lo_others = half * (1 - lo), half * lo
    cut = half * 2 // 5

    def columns_at(first_, count):
        return pl.ds(pl.multiple_of(first_, 128), count)

    def forward(slot, first_, count, where):
        c = columns_at(first_, count)
        return start(bb.at[slot, :, c], bb.at[D, :, c], to[where])

    first = []
    for o in range(2):
        r = slice(o * slab, (o + 1) * slab)
        first.append((
            start(b_hbm.at[r, others], bb.at[X, r, others], to[X]),
            start(b_hbm.at[r, mine], bb.at[F, r, mine], to[R]),
            start(b_hbm.at[r, others], bb.at[R, r, others], to[F]),
        ))
    smalls = [
        start(small.at[ME], small.at[slot], to[back])
        for slot, back in ((X, X), (F, R), (R, F), (D, D))
    ]

    def pair_sums(lo_, hi_):
        for n in range(lo_, hi_):
            kind, u, v = BLOCKS[n]
            one, two = KINDS[kind]
            swap = 1 - lo if kind == KR else lo
            columns = others if kind == KR else mine
            head, tail = one + swap * (two - one), two + swap * (one - two)
            a_at = pl.multiple_of((u + swap * (v - u)) * slab, slab)
            b_at = pl.multiple_of((v + swap * (u - v)) * slab, slab)
            a = bb[head, pl.ds(a_at, slab), columns]
            b = bb[tail, pl.ds(b_at, slab), columns]
            direct = lax.dot_general(a + a, b, NT, preferred_element_type=F32)
            exchanged = lax.dot_general(b, a, NT, preferred_element_type=F32)
            k[n] = direct - exchanged

    my_half = pl.ds(pl.multiple_of(core * crows, crows), crows)
    its_half = pl.ds(pl.multiple_of(other_core * crows, crows), crows)

    def to_other_core(lo_, hi_):
        return start(k.at[lo_:hi_, its_half], rc.at[lo_:hi_], to_core)

    def sum_cores(lo_, hi_, shift):
        for n in range(lo_, hi_):
            total = k[n, my_half] + rc[n]
            k[n, my_half] = total
            top = jnp.max(jnp.max(jnp.abs(total), axis=0, keepdims=True), axis=1, keepdims=True)
            top = jnp.maximum(top, 1e-30)
            q[n] = jnp.round(total * (TOP / top)).astype(jnp.int32).astype(I16)
            scale[n + shift:n + shift + 1] = jnp.broadcast_to(top * (1.0 / TOP), (1, 128))

    def along_y(batch):
        lo_, hi_ = SPANS[batch]
        s_lo, s_hi = SCALES[batch]
        out = []
        for j, y_ in enumerate((y1, y2, y3)):
            r = pl.ds(pl.multiple_of(y_ * yrows, yrows), yrows)
            out.append(start(scale.at[s_lo:s_hi], ry_scale.at[j, s_lo:s_hi], to_y[j]))
            out.append(start(q.at[lo_:hi_, r], ry.at[j, lo_:hi_], to_y[j]))
        return out

    def sum_y(batch, copies):
        for c in copies:
            c.wait_recv()
        lo_, hi_ = SPANS[batch]
        r = pl.ds(pl.multiple_of(core * crows + y * yrows, yrows), yrows)
        for n in range(lo_, hi_):
            total = k[n, r]
            for j in range(3):
                total += ry[j, n].astype(jnp.int32).astype(F32) * ry_scale[j, n + batch:n + batch + 1, 0:1]
            ys[n] = total
        x_rows = pl.ds(pl.multiple_of(other_xh * rows, rows), rows)
        return start(ys.at[lo_:hi_, x_rows], rx.at[lo_:hi_], to_xh)

    def sum_x(batch, c):
        c.wait_recv()
        lo_, hi_ = SPANS[batch]
        p[lo_:hi_] = ys[lo_:hi_, pl.ds(pl.multiple_of(xh * rows, rows), rows)] + rx[lo_:hi_]
        out = []
        for (a_, b_), dst, where in ((TO_X[batch], cx, to[X]), (TO_F[batch], cr, to[F]), (TO_R[batch], cf, to[R])):
            out.append(start(p.at[a_:b_], dst.at[a_:b_], where))
        return out

    own.wait()
    for c in first[0]:
        c.wait_recv()
    pair_sums(SPANS[0][0], CUT[0])
    core0 = [to_other_core(SPANS[0][0], CUT[0])]
    pair_sums(CUT[0], SPANS[0][1])
    core0.append(to_other_core(CUT[0], SPANS[0][1]))
    core0[0].wait_recv()
    sum_cores(SPANS[0][0], CUT[0], 0)
    core0[1].wait_recv()
    sum_cores(CUT[0], SPANS[0][1], 0)
    y_0 = along_y(0)
    for c in first[1]:
        c.wait_recv()
    second = [
        start(b_hbm.at[:, mine], bb.at[X, :, mine], to[X]),
        start(b_hbm.at[:, others], bb.at[F, :, others], to[R]),
        start(b_hbm.at[:, mine], bb.at[R, :, mine], to[F]),
    ]
    pair_sums(SPANS[1][0], CUT[1])
    core1 = [to_other_core(SPANS[1][0], CUT[1])]
    pair_sums(CUT[1], SPANS[1][1])
    core1.append(to_other_core(CUT[1], SPANS[1][1]))
    core1[0].wait_recv()
    sum_cores(SPANS[1][0], CUT[1], 1)
    core1[1].wait_recv()
    sum_cores(CUT[1], SPANS[1][1], 1)
    y_1 = along_y(1)
    x_0 = sum_y(0, y_0)
    x_1 = sum_y(1, y_1)
    place_0 = sum_x(0, x_0)
    diagonal = [forward(X, lo_mine, cut, F)]
    for c in smalls:
        c.wait_recv()
    place_1 = sum_x(1, x_1)
    for c in place_0 + place_1:
        c.wait_recv()

    second[0].wait_recv()
    diagonal += [forward(X, lo_mine + cut, half - cut, F), forward(X, lo_others, cut, F)]

    my_rows = pl.ds(pl.multiple_of(my_row, rows), rows)
    for pair in (X, F, R, D):
        swap = lo if pair in (X, F) else 1 - lo
        flag_row = 2 if pair in (X, D) else 3
        flag = small[ME + swap * (pair - ME), flag_row:flag_row + 1]
        for i in range(2):
            for j in range(2):
                if pair == X:
                    total = p[AT[KX, i, j]] + cx[AT[KX, j, i]]
                elif pair == F:
                    total = p[AT[KF, i, j]] + cf[AT[KR, j, i]]
                elif pair == R:
                    total = p[AT[KR, i, j]] + cr[AT[KF, j, i]]
                else:
                    total = cx[AT[KXF, i, j]] + cr[AT[KXF, j, i]]
                energy = small[ME, i:i + 1] + small[pair, j:j + 1]
                t[2 * pair + i, my_rows, j * slab:(j + 1) * slab] = (flag * total / (energy - virtual)).astype(BF16)

    to_y1, _, to_y3 = to_y

    def spread(part, core_, y_, xh_, where):
        r = pl.ds(pl.multiple_of(core_ * crows + y_ * yrows + xh_ * rows, rows), rows)
        source = t.at[4 * part:4 * part + 4, r]
        return start(source, source, where)

    own_part, near, far, last = [], [], [], []
    for h in range(2):
        own_part.append((
            spread(h, core, y, xh, to_xh),
            spread(h, core, y, xh, to_y3),
            spread(h, core, y, xh, to_y1),
            spread(h, core, y, xh, to_core),
        ))
    for h in range(2):
        own_part[h][0].wait_recv()
        near.append((
            spread(h, core, y, other_xh, to_y3),
            spread(h, core, y, other_xh, to_y1),
            spread(h, core, y, other_xh, to_core),
        ))
        own_part[h][1].wait_recv()
        far.append([spread(h, core, y3, xh, to_y1), spread(h, core, y3, xh, to_core)])
        own_part[h][2].wait_recv()
        far[h].append(spread(h, core, y1, xh, to_core))
    diagonal.append(forward(F, lo_mine + cut, half - cut, X))
    for h in range(2):
        near[h][1].wait_recv()
        far[h] += [spread(h, core, y1, other_xh, to_y3), spread(h, core, y1, other_xh, to_core)]
        near[h][0].wait_recv()
        far[h].append(spread(h, core, y3, other_xh, to_core))
    for h in range(2):
        far[h][0].wait_recv()
        last.append([spread(h, core, y2, xh, to_core)])
        far[h][3].wait_recv()
        last[h].append(spread(h, core, y2, other_xh, to_core))

    def orient(h):
        for c in (own_part[h][3], near[h][2], far[h][1], far[h][2], far[h][4], far[h][5], last[h][0], last[h][1]):
            c.wait_recv()

        @pl.when(lo == h)
        def _():
            tt[4 * h:4 * h + 4] = t[4 * h:4 * h + 4]

        @pl.when(lo != h)
        def _():
            for n in range(4 * h, 4 * h + 4):
                for j in range(2):
                    tt[n, :, j * slab:(j + 1) * slab] = t[n, :, j * slab:(j + 1) * slab].T

    pieces = ((lo_mine, cut), (lo_mine + cut, half - cut), (lo_others, cut), (lo_others + cut, half - cut))

    def apply(slots, piece, earlier):
        c = columns_at(*piece)
        out = []
        for i in range(2):
            total = earlier(i)
            for slot in slots:
                term = jnp.dot(tt[2 * slot + i], bb[slot, :, c], preferred_element_type=F32)
                total = term if total is None else total + term
            out.append(total)
        return out

    orient(0)
    second[1].wait_recv()
    at = 0
    for piece in pieces:
        for i, total in enumerate(apply((X, F), piece, lambda i: None)):
            g[i * slab:(i + 1) * slab, at:at + piece[1]] = total
        at += piece[1]
    orient(1)
    second[2].wait_recv()
    at = 0
    results = []
    for n, piece in enumerate(pieces):
        diagonal[n].wait_recv()
        here = slice(at, at + piece[1])
        for i, total in enumerate(apply((R, D), piece, lambda i: g[i * slab:(i + 1) * slab, here])):
            g[i * slab:(i + 1) * slab, here] = total
        result = pltpu.make_async_copy(g.at[:, here], out_hbm.at[:, columns_at(*piece)], out_sem.at[n])
        result.start()
        results.append(result)
        at += piece[1]
    for c in started:
        c.wait_send()
    for c in results:
        c.wait()


def on_device(planes, orbital_factors, occ_energy, vir_energy, pair_kept):
    occ_dev, slab, aux_dev = orbital_factors.shape
    width = occ_dev * slab
    rows = slab // 16
    copies = 72
    gamma = pl.pallas_call(
        functools.partial(kernel, planes),
        out_shape=jax.ShapeDtypeStruct((width, aux_dev), F32),
        in_specs=[pl.BlockSpec(memory_space=pltpu.HBM)] + [pl.BlockSpec(memory_space=pltpu.VMEM)] * 3,
        out_specs=pl.BlockSpec(memory_space=pl.ANY),
        scratch_shapes=[
            pltpu.VMEM((5, width, aux_dev), BF16),
            pltpu.VMEM((5, 8, slab), F32),
            pltpu.VMEM((16, slab, slab), F32),
            pltpu.VMEM((16, slab // 2, slab), F32),
            pltpu.VMEM((16, slab // 2, slab), I16),
            pltpu.VMEM((24, 128), F32),
            pltpu.VMEM((3, 16, slab // 8, slab), I16),
            pltpu.VMEM((3, 24, 128), F32),
            pltpu.VMEM((16, slab // 8, slab), F32),
            pltpu.VMEM((16, rows, slab), F32),
            pltpu.VMEM((16, rows, slab), F32),
            pltpu.VMEM((16, rows, slab), F32),
            pltpu.VMEM((16, rows, slab), F32),
            pltpu.VMEM((16, rows, slab), F32),
            pltpu.VMEM((8, slab, width), BF16),
            pltpu.VMEM((8, slab, width), BF16),
            pltpu.VMEM((width, aux_dev), F32),
            pltpu.SemaphoreType.DMA((copies,)),
            pltpu.SemaphoreType.DMA((copies,)),
            pltpu.SemaphoreType.DMA((1,)),
            pltpu.SemaphoreType.DMA((4,)),
        ],
        compiler_params=pltpu.CompilerParams(
            collective_id=0, has_side_effects=True, vmem_limit_bytes=60 * 1024 * 1024
        ),
        cost_estimate=pl.CostEstimate(
            flops=12 * width * width * aux_dev, bytes_accessed=6 * width * aux_dev, transcendentals=0
        ),
    )(orbital_factors.reshape(width, aux_dev), occ_energy.reshape(1, 2), vir_energy.reshape(1, slab), pair_kept)
    return gamma.reshape(occ_dev, slab, aux_dev)


def solution(mesh):
    in_specs = (P("occ", None, "aux"), P("occ"), P(), P("occ", None))
    out_specs = P("occ", None, "aux")
    return jax.shard_map(
        functools.partial(on_device, mesh.shape["occ"] // 2),
        mesh=mesh, in_specs=in_specs, out_specs=out_specs, check_vma=False,
    )
```

time: 313 us -> 82.9 us (0.26)
  the two profiles are of different devices: /device:TPU:2 before, /device:TPU:1 now
where the time goes in v2:
time: 82.9 us; the launch traced here: 82.8 us
  Pallas kernels  79.4 us (96%)
  local copies, waits for them, and re-layouts  3.4 us (4%)
    pallas_call x1, Pallas kernels, on_device(): pl.pallas_call(functools.partial(kernel, planes), out_shape=jax.ShapeDtyp...  79.4 us
    unnamed x1, local copies, waits for them, and re-layouts  3.4 us

profile of v2, /device:TPU:1, one launch (start us, length us, event | category | flops | bytes accessed | tf_op | source)
XLA Modules:
  0.0 82.8 jit_solution(364325456883238355)
XLA Ops:
  0.0 79.4 %shard_map.46 = f32[512,1280]{1,0:T(8,128)} custom-call(bf16[512,1280]{1,0:T(8,128)(2,1)} %bitcast.5, bf16[1,2]{1,0:T(2,128)(2,1)} %bitcast.7, f32[1,256]{1,0:T(1,128)} %bitcast.6, s32[1,2]{1,0:T(1,128)} %kept_ref.1), custom_call_target="tpu_custom_call" | custom-call | flops 4026531840 | bytes 3932160 | tf_op jit(solution)/shard_map/pallas_call | solution.py:335
  79.4 3.4 %copy.6 = f32[2,256,1280]{2,1,0:T(8,128)} copy(f32[2,256,1280]{2,1,0:T(8,128)} %bitcast.4) | data formatting | bytes 5242880

commit v3 on v2

--- a/solution.py
+++ b/solution.py
@@ -18,21 +18,21 @@
 KX, KXF, KF, KR = range(4)
 BATCHES = (
     ((KX, 0, 0), (KX, 1, 0), (KXF, 0, 0), (KF, 0, 0), (KF, 1, 0), (KR, 0, 0), (KR, 1, 0)),
-    ((KX, 0, 1), (KX, 1, 1), (KXF, 0, 1), (KXF, 1, 0), (KXF, 1, 1), (KF, 0, 1), (KF, 1, 1), (KR, 0, 1), (KR, 1, 1)),
+    ((KX, 0, 1), (KX, 1, 1), (KXF, 0, 1), (KXF, 1, 0), (KXF, 1, 1)),
+    ((KF, 0, 1), (KF, 1, 1), (KR, 0, 1), (KR, 1, 1)),
 )
-BLOCKS = BATCHES[0] + BATCHES[1]
+BLOCKS = BATCHES[0] + BATCHES[1] + BATCHES[2]
 AT = {block: n for n, block in enumerate(BLOCKS)}
-SPANS = ((0, 7), (7, 16))
-TO_X = ((0, 3), (7, 12))
-TO_F = ((2, 5), (9, 14))
-TO_R = ((5, 7), (14, 16))
-CUT = (3, 12)
-SCALES = ((0, 8), (8, 24))
+SPANS = ((0, 7), (7, 12), (12, 16))
+TO_X = ((0, 3), (7, 12), None)
+TO_F = ((2, 5), (9, 12), (12, 14))
+TO_R = ((5, 7), None, (14, 16))
+ORDER = (X, D, F, R)
 
 
 def kernel(
-    planes, b_hbm, e_ref, v_ref, kept_ref, out_hbm,
-    bb, small, k, rc, q, scale, ry, ry_scale, ys, rx, p, cx, cr, cf, t, tt, g,
+    planes, b_hbm, e_hbm, v_hbm, kept_hbm, out_hbm,
+    bb, e_ref, v_ref, kept_ref, small, k, rc, q, scale, ry, ry_scale, ys, rx, p, cx, cr, cf, t, tt, g,
     send, recv, local, out_sem,
 ):
     slab = k.shape[1]
@@ -74,10 +74,48 @@
 
     own = pltpu.make_async_copy(b_hbm, bb.at[ME], local.at[0])
     own.start()
+    arguments = [
+        pltpu.make_async_copy(src, dst, local.at[1 + n])
+        for n, (src, dst) in enumerate(((e_hbm, e_ref), (v_hbm, v_ref), (kept_hbm, kept_ref)))
+    ]
+    for c in arguments:
+        c.start()
     barrier = pltpu.get_barrier_semaphore()
     for where in (*to, to_core, *to_y, to_xh):
         pl.semaphore_signal(barrier, inc=1, device_id=device(where), device_id_type=pl.DeviceIdType.MESH)
 
+    pl.semaphore_wait(barrier, 9)
+
+    mine = pl.ds(pl.multiple_of(half * (1 - lo), half), half)
+    others = pl.ds(pl.multiple_of(half * lo, half), half)
+
+    lo_mine, lo_others = half * (1 - lo), half * lo
+    cut = half * 2 // 5
+    rest = half - cut
+
+    def columns_at(first_, count):
+        return pl.ds(pl.multiple_of(first_, 128), count)
+
+    def forward(slot, first_, count, where):
+        c = columns_at(first_, count)
+        return start(bb.at[slot, :, c], bb.at[D, :, c], to[where])
+
+    first = []
+    for o in range(2):
+        r = slice(o * slab, (o + 1) * slab)
+        first.append((
+            start(b_hbm.at[r, others], bb.at[X, r, others], to[X]),
+            start(b_hbm.at[r, mine], bb.at[F, r, mine], to[R]),
+            start(b_hbm.at[r, others], bb.at[R, r, others], to[F]),
+        ))
+    second = [
+        start(b_hbm.at[:, mine], bb.at[X, :, mine], to[X]),
+        start(b_hbm.at[:, others], bb.at[F, :, others], to[R]),
+        start(b_hbm.at[:, mine], bb.at[R, :, mine], to[F]),
+    ]
+
+    for c in arguments:
+        c.wait()
     for i in range(2):
         small[ME, i:i + 1] = jnp.broadcast_to(e_ref[:, i:i + 1].astype(F32), (1, slab))
         small[ME, 2 + i:3 + i] = jnp.broadcast_to(kept_ref[:, i:i + 1].astype(F32), (1, slab))
@@ -87,29 +125,6 @@
     mine_v = jnp.sum(jnp.where(spot == my_row, v_ref[...], 0.0), axis=1, keepdims=True)
     virtual = mine_v + v_ref[...]
 
-    pl.semaphore_wait(barrier, 9)
-
-    mine = pl.ds(pl.multiple_of(half * (1 - lo), half), half)
-    others = pl.ds(pl.multiple_of(half * lo, half), half)
-
-    lo_mine, lo_others = half * (1 - lo), half * lo
-    cut = half * 2 // 5
-
-    def columns_at(first_, count):
-        return pl.ds(pl.multiple_of(first_, 128), count)
-
-    def forward(slot, first_, count, where):
-        c = columns_at(first_, count)
-        return start(bb.at[slot, :, c], bb.at[D, :, c], to[where])
-
-    first = []
-    for o in range(2):
-        r = slice(o * slab, (o + 1) * slab)
-        first.append((
-            start(b_hbm.at[r, others], bb.at[X, r, others], to[X]),
-            start(b_hbm.at[r, mine], bb.at[F, r, mine], to[R]),
-            start(b_hbm.at[r, others], bb.at[R, r, others], to[F]),
-        ))
     smalls = [
         start(small.at[ME], small.at[slot], to[back])
         for slot, back in ((X, X), (F, R), (R, F), (D, D))
@@ -136,22 +151,23 @@
     def to_other_core(lo_, hi_):
         return start(k.at[lo_:hi_, its_half], rc.at[lo_:hi_], to_core)
 
-    def sum_cores(lo_, hi_, shift):
+    def sum_cores(batch, lo_, hi_):
         for n in range(lo_, hi_):
             total = k[n, my_half] + rc[n]
             k[n, my_half] = total
             top = jnp.max(jnp.max(jnp.abs(total), axis=0, keepdims=True), axis=1, keepdims=True)
             top = jnp.maximum(top, 1e-30)
             q[n] = jnp.round(total * (TOP / top)).astype(jnp.int32).astype(I16)
-            scale[n + shift:n + shift + 1] = jnp.broadcast_to(top * (1.0 / TOP), (1, 128))
+            row = 8 * batch + n - SPANS[batch][0]
+            scale[row:row + 1] = jnp.broadcast_to(top * (1.0 / TOP), (1, 128))
 
     def along_y(batch):
         lo_, hi_ = SPANS[batch]
-        s_lo, s_hi = SCALES[batch]
+        s = slice(8 * batch, 8 * batch + 8)
         out = []
         for j, y_ in enumerate((y1, y2, y3)):
             r = pl.ds(pl.multiple_of(y_ * yrows, yrows), yrows)
-            out.append(start(scale.at[s_lo:s_hi], ry_scale.at[j, s_lo:s_hi], to_y[j]))
+            out.append(start(scale.at[s], ry_scale.at[j, s], to_y[j]))
             out.append(start(q.at[lo_:hi_, r], ry.at[j, lo_:hi_], to_y[j]))
         return out
 
@@ -161,9 +177,10 @@
         lo_, hi_ = SPANS[batch]
         r = pl.ds(pl.multiple_of(core * crows + y * yrows, yrows), yrows)
         for n in range(lo_, hi_):
+            row = 8 * batch + n - lo_
             total = k[n, r]
             for j in range(3):
-                total += ry[j, n].astype(jnp.int32).astype(F32) * ry_scale[j, n + batch:n + batch + 1, 0:1]
+                total += ry[j, n].astype(jnp.int32).astype(F32) * ry_scale[j, row:row + 1, 0:1]
             ys[n] = total
         x_rows = pl.ds(pl.multiple_of(other_xh * rows, rows), rows)
         return start(ys.at[lo_:hi_, x_rows], rx.at[lo_:hi_], to_xh)
@@ -173,53 +190,49 @@
         lo_, hi_ = SPANS[batch]
         p[lo_:hi_] = ys[lo_:hi_, pl.ds(pl.multiple_of(xh * rows, rows), rows)] + rx[lo_:hi_]
         out = []
-        for (a_, b_), dst, where in ((TO_X[batch], cx, to[X]), (TO_F[batch], cr, to[F]), (TO_R[batch], cf, to[R])):
-            out.append(start(p.at[a_:b_], dst.at[a_:b_], where))
+        for span, dst, where in ((TO_X[batch], cx, to[X]), (TO_F[batch], cr, to[F]), (TO_R[batch], cf, to[R])):
+            if span is not None:
+                out.append(start(p.at[slice(*span)], dst.at[slice(*span)], where))
         return out
 
     own.wait()
     for c in first[0]:
         c.wait_recv()
-    pair_sums(SPANS[0][0], CUT[0])
-    core0 = [to_other_core(SPANS[0][0], CUT[0])]
-    pair_sums(CUT[0], SPANS[0][1])
-    core0.append(to_other_core(CUT[0], SPANS[0][1]))
+    pair_sums(0, 3)
+    core0 = [to_other_core(0, 3)]
+    pair_sums(3, 7)
+    core0.append(to_other_core(3, 7))
     core0[0].wait_recv()
-    sum_cores(SPANS[0][0], CUT[0], 0)
+    sum_cores(0, 0, 3)
     core0[1].wait_recv()
-    sum_cores(CUT[0], SPANS[0][1], 0)
+    sum_cores(0, 3, 7)
     y_0 = along_y(0)
     for c in first[1]:
         c.wait_recv()
-    second = [
-        start(b_hbm.at[:, mine], bb.at[X, :, mine], to[X]),
-        start(b_hbm.at[:, others], bb.at[F, :, others], to[R]),
-        start(b_hbm.at[:, mine], bb.at[R, :, mine], to[F]),
-    ]
-    pair_sums(SPANS[1][0], CUT[1])
-    core1 = [to_other_core(SPANS[1][0], CUT[1])]
-    pair_sums(CUT[1], SPANS[1][1])
-    core1.append(to_other_core(CUT[1], SPANS[1][1]))
-    core1[0].wait_recv()
-    sum_cores(SPANS[1][0], CUT[1], 1)
-    core1[1].wait_recv()
-    sum_cores(CUT[1], SPANS[1][1], 1)
+    pair_sums(*SPANS[1])
+    core1 = to_other_core(*SPANS[1])
+    pair_sums(*SPANS[2])
+    core2 = to_other_core(*SPANS[2])
+    core1.wait_recv()
+    sum_cores(1, *SPANS[1])
     y_1 = along_y(1)
+    core2.wait_recv()
+    sum_cores(2, *SPANS[2])
+    y_2 = along_y(2)
     x_0 = sum_y(0, y_0)
     x_1 = sum_y(1, y_1)
+    x_2 = sum_y(2, y_2)
+    diagonal = [forward(X, lo_mine, cut, F)]
     place_0 = sum_x(0, x_0)
-    diagonal = [forward(X, lo_mine, cut, F)]
-    for c in smalls:
-        c.wait_recv()
     place_1 = sum_x(1, x_1)
-    for c in place_0 + place_1:
-        c.wait_recv()
+    place_2 = sum_x(2, x_2)
 
     second[0].wait_recv()
-    diagonal += [forward(X, lo_mine + cut, half - cut, F), forward(X, lo_others, cut, F)]
+    diagonal += [forward(X, lo_mine + cut, rest, F), forward(X, lo_others, cut, F)]
 
     my_rows = pl.ds(pl.multiple_of(my_row, rows), rows)
-    for pair in (X, F, R, D):
+
+    def finish(pair):
         swap = lo if pair in (X, F) else 1 - lo
         flag_row = 2 if pair in (X, D) else 3
         flag = small[ME + swap * (pair - ME), flag_row:flag_row + 1]
@@ -234,7 +247,8 @@
                 else:
                     total = cx[AT[KXF, i, j]] + cr[AT[KXF, j, i]]
                 energy = small[ME, i:i + 1] + small[pair, j:j + 1]
-                t[2 * pair + i, my_rows, j * slab:(j + 1) * slab] = (flag * total / (energy - virtual)).astype(BF16)
+                row = 2 * ORDER.index(pair) + i
+                t[row, my_rows, j * slab:(j + 1) * slab] = (flag * total / (energy - virtual)).astype(BF16)
 
     to_y1, _, to_y3 = to_y
 
@@ -244,7 +258,14 @@
         return start(source, source, where)
 
     own_part, near, far, last = [], [], [], []
+    for c in smalls + place_0 + place_1:
+        c.wait_recv()
     for h in range(2):
+        if h == 1:
+            for c in place_2:
+                c.wait_recv()
+        finish(ORDER[2 * h])
+        finish(ORDER[2 * h + 1])
         own_part.append((
             spread(h, core, y, xh, to_xh),
             spread(h, core, y, xh, to_y3),
@@ -262,7 +283,7 @@
         far.append([spread(h, core, y3, xh, to_y1), spread(h, core, y3, xh, to_core)])
         own_part[h][2].wait_recv()
         far[h].append(spread(h, core, y1, xh, to_core))
-    diagonal.append(forward(F, lo_mine + cut, half - cut, X))
+    diagonal.append(forward(F, lo_mine + cut, rest, X))
     for h in range(2):
         near[h][1].wait_recv()
         far[h] += [spread(h, core, y1, other_xh, to_y3), spread(h, core, y1, other_xh, to_core)]
@@ -278,17 +299,19 @@
         for c in (own_part[h][3], near[h][2], far[h][1], far[h][2], far[h][4], far[h][5], last[h][0], last[h][1]):
             c.wait_recv()
 
-        @pl.when(lo == h)
-        def _():
-            tt[4 * h:4 * h + 4] = t[4 * h:4 * h + 4]
-
-        @pl.when(lo != h)
-        def _():
-            for n in range(4 * h, 4 * h + 4):
+        for n in range(4 * h, 4 * h + 4):
+            second_at = 1 if ORDER[n // 2] in (X, F) else 0
+
+            @pl.when(lo != second_at)
+            def _(n=n):
+                tt[n] = t[n]
+
+            @pl.when(lo == second_at)
+            def _(n=n):
                 for j in range(2):
                     tt[n, :, j * slab:(j + 1) * slab] = t[n, :, j * slab:(j + 1) * slab].T
 
-    pieces = ((lo_mine, cut), (lo_mine + cut, half - cut), (lo_others, cut), (lo_others + cut, half - cut))
+    pieces = ((lo_mine, cut), (lo_mine + cut, rest), (lo_others, cut), (lo_others + cut, rest))
 
     def apply(slots, piece, earlier):
         c = columns_at(*piece)
@@ -296,26 +319,30 @@
         for i in range(2):
             total = earlier(i)
             for slot in slots:
-                term = jnp.dot(tt[2 * slot + i], bb[slot, :, c], preferred_element_type=F32)
+                term = jnp.dot(tt[2 * ORDER.index(slot) + i], bb[slot, :, c], preferred_element_type=F32)
                 total = term if total is None else total + term
             out.append(total)
         return out
 
     orient(0)
-    second[1].wait_recv()
     at = 0
-    for piece in pieces:
-        for i, total in enumerate(apply((X, F), piece, lambda i: None)):
+    for n, piece in enumerate(pieces):
+        if n < 2:
+            diagonal[n].wait_recv()
+        for i, total in enumerate(apply((X, D) if n < 2 else (X,), piece, lambda i: None)):
             g[i * slab:(i + 1) * slab, at:at + piece[1]] = total
         at += piece[1]
     orient(1)
+    second[1].wait_recv()
     second[2].wait_recv()
     at = 0
     results = []
     for n, piece in enumerate(pieces):
-        diagonal[n].wait_recv()
         here = slice(at, at + piece[1])
-        for i, total in enumerate(apply((R, D), piece, lambda i: g[i * slab:(i + 1) * slab, here])):
+        if n >= 2:
+            diagonal[n].wait_recv()
+        slots = (F, R) if n < 2 else (F, R, D)
+        for i, total in enumerate(apply(slots, piece, lambda i: g[i * slab:(i + 1) * slab, here])):
             g[i * slab:(i + 1) * slab, here] = total
         result = pltpu.make_async_copy(g.at[:, here], out_hbm.at[:, columns_at(*piece)], out_sem.at[n])
         result.start()
@@ -331,14 +358,17 @@
     occ_dev, slab, aux_dev = orbital_factors.shape
     width = occ_dev * slab
     rows = slab // 16
-    copies = 72
+    copies = 79
     gamma = pl.pallas_call(
         functools.partial(kernel, planes),
         out_shape=jax.ShapeDtypeStruct((width, aux_dev), F32),
-        in_specs=[pl.BlockSpec(memory_space=pltpu.HBM)] + [pl.BlockSpec(memory_space=pltpu.VMEM)] * 3,
+        in_specs=[pl.BlockSpec(memory_space=pl.ANY)] * 4,
         out_specs=pl.BlockSpec(memory_space=pl.ANY),
         scratch_shapes=[
             pltpu.VMEM((5, width, aux_dev), BF16),
+            pltpu.VMEM((1, 2), BF16),
+            pltpu.VMEM((1, slab), F32),
+            pltpu.VMEM((1, 2), jnp.int32),
             pltpu.VMEM((5, 8, slab), F32),
             pltpu.VMEM((16, slab, slab), F32),
             pltpu.VMEM((16, slab // 2, slab), F32),
@@ -357,7 +387,7 @@
             pltpu.VMEM((width, aux_dev), F32),
             pltpu.SemaphoreType.DMA((copies,)),
             pltpu.SemaphoreType.DMA((copies,)),
-            pltpu.SemaphoreType.DMA((1,)),
+            pltpu.SemaphoreType.DMA((4,)),
             pltpu.SemaphoreType.DMA((4,)),
         ],
         compiler_params=pltpu.CompilerParams(

time: 82.9 us -> 77.3 us (0.932)
  Pallas kernels: 79.4 us -> 73.8 us
    pallas_call x1, Pallas kernels: 79.4 us -> 73.8 us  [on_device(): pl.pallas_call(functools.partial(kernel, planes), out_shape=jax.ShapeDtyp...]
where the time goes in v3:
time: 77.3 us; the launch traced here: 77.2 us
  Pallas kernels  73.8 us (95%)
  local copies, waits for them, and re-layouts  3.4 us (4%)
    pallas_call x1, Pallas kernels, on_device(): pl.pallas_call(functools.partial(kernel, planes), out_shape=jax.ShapeDtyp...  73.8 us
    unnamed x1, local copies, waits for them, and re-layouts  3.4 us

profile of v3, /device:TPU:1, one launch (start us, length us, event | category | flops | bytes accessed | tf_op | source)
XLA Modules:
  0.0 77.2 jit_solution(2581832230232142210)
XLA Ops:
  0.0 73.8 %shard_map.46 = f32[512,1280]{1,0:T(8,128)} custom-call(bf16[512,1280]{1,0:T(8,128)(2,1)} %bitcast.5, bf16[1,2]{1,0:T(2,128)(2,1)} %bitcast.7, f32[1,256]{1,0:T(1,128)} %bitcast.6, s32[1,2]{1,0:T(1,128)} %kept_hbm.1), custom_call_target="tpu_custom_call" | custom-call | flops 4026531840 | bytes 3932160 | tf_op jit(solution)/shard_map/pallas_call | solution.py:362
  73.8 3.4 %copy.6 = f32[2,256,1280]{2,1,0:T(8,128)} copy(f32[2,256,1280]{2,1,0:T(8,128)} %bitcast.4) | data formatting | bytes 5242880

commit v4 on v3

--- a/solution.py
+++ b/solution.py
@@ -100,6 +100,10 @@
         c = columns_at(first_, count)
         return start(bb.at[slot, :, c], bb.at[D, :, c], to[where])
 
+    def own_to_x(first_, count):
+        c = columns_at(first_, count)
+        return start(b_hbm.at[:, c], bb.at[X, :, c], to[X])
+
     first = []
     for o in range(2):
         r = slice(o * slab, (o + 1) * slab)
@@ -109,7 +113,7 @@
             start(b_hbm.at[r, others], bb.at[R, r, others], to[F]),
         ))
     second = [
-        start(b_hbm.at[:, mine], bb.at[X, :, mine], to[X]),
+        own_to_x(lo_mine, rest),
         start(b_hbm.at[:, others], bb.at[F, :, others], to[R]),
         start(b_hbm.at[:, mine], bb.at[R, :, mine], to[F]),
     ]
@@ -219,14 +223,14 @@
     core2.wait_recv()
     sum_cores(2, *SPANS[2])
     y_2 = along_y(2)
+    diagonal = [forward(X, lo_mine, cut, F)]
     x_0 = sum_y(0, y_0)
     x_1 = sum_y(1, y_1)
+    place_0 = sum_x(0, x_0)
     x_2 = sum_y(2, y_2)
-    diagonal = [forward(X, lo_mine, cut, F)]
-    place_0 = sum_x(0, x_0)
     place_1 = sum_x(1, x_1)
+    second.append(own_to_x(lo_mine + rest, cut))
     place_2 = sum_x(2, x_2)
-
     second[0].wait_recv()
     diagonal += [forward(X, lo_mine + cut, rest, F), forward(X, lo_others, cut, F)]
 
@@ -250,14 +254,12 @@
                 row = 2 * ORDER.index(pair) + i
                 t[row, my_rows, j * slab:(j + 1) * slab] = (flag * total / (energy - virtual)).astype(BF16)
 
-    to_y1, _, to_y3 = to_y
-
     def spread(part, core_, y_, xh_, where):
         r = pl.ds(pl.multiple_of(core_ * crows + y_ * yrows + xh_ * rows, rows), rows)
         source = t.at[4 * part:4 * part + 4, r]
         return start(source, source, where)
 
-    own_part, near, far, last = [], [], [], []
+    own_part, near, far = [], [], [[], []]
     for c in smalls + place_0 + place_1:
         c.wait_recv()
     for h in range(2):
@@ -266,37 +268,19 @@
                 c.wait_recv()
         finish(ORDER[2 * h])
         finish(ORDER[2 * h + 1])
-        own_part.append((
-            spread(h, core, y, xh, to_xh),
-            spread(h, core, y, xh, to_y3),
-            spread(h, core, y, xh, to_y1),
-            spread(h, core, y, xh, to_core),
-        ))
+        own_part.append([spread(h, core, y, xh, where) for where in (to_xh, to_core, to_y[1], to_y[0], to_y[2])])
     for h in range(2):
         own_part[h][0].wait_recv()
-        near.append((
-            spread(h, core, y, other_xh, to_y3),
-            spread(h, core, y, other_xh, to_y1),
-            spread(h, core, y, other_xh, to_core),
-        ))
-        own_part[h][1].wait_recv()
-        far.append([spread(h, core, y3, xh, to_y1), spread(h, core, y3, xh, to_core)])
-        own_part[h][2].wait_recv()
-        far[h].append(spread(h, core, y1, xh, to_core))
+        near.append([spread(h, core, y, other_xh, where) for where in (to_core, to_y[1], to_y[0], to_y[2])])
     diagonal.append(forward(F, lo_mine + cut, rest, X))
-    for h in range(2):
-        near[h][1].wait_recv()
-        far[h] += [spread(h, core, y1, other_xh, to_y3), spread(h, core, y1, other_xh, to_core)]
-        near[h][0].wait_recv()
-        far[h].append(spread(h, core, y3, other_xh, to_core))
-    for h in range(2):
-        far[h][0].wait_recv()
-        last.append([spread(h, core, y2, xh, to_core)])
-        far[h][3].wait_recv()
-        last[h].append(spread(h, core, y2, other_xh, to_core))
+    for copies, skip, xh_ in ((own_part, 2, xh), (near, 1, other_xh)):
+        for h in range(2):
+            for c, y_ in ((copies[h][skip + 1], y1), (copies[h][skip + 2], y3), (copies[h][skip], y2)):
+                c.wait_recv()
+                far[h].append(spread(h, core, y_, xh_, to_core))
 
     def orient(h):
-        for c in (own_part[h][3], near[h][2], far[h][1], far[h][2], far[h][4], far[h][5], last[h][0], last[h][1]):
+        for c in (own_part[h][1], near[h][0], *far[h]):
             c.wait_recv()
 
         for n in range(4 * h, 4 * h + 4):
@@ -325,6 +309,7 @@
         return out
 
     orient(0)
+    second[3].wait_recv()
     at = 0
     for n, piece in enumerate(pieces):
         if n < 2:
@@ -358,7 +343,7 @@
     occ_dev, slab, aux_dev = orbital_factors.shape
     width = occ_dev * slab
     rows = slab // 16
-    copies = 79
+    copies = 80
     gamma = pl.pallas_call(
         functools.partial(kernel, planes),
         out_shape=jax.ShapeDtypeStruct((width, aux_dev), F32),

time: 77.3 us -> 75.6 us (0.978)
  Pallas kernels: 73.8 us -> 72 us
    pallas_call x1, Pallas kernels: 73.8 us -> 72 us  [on_device(): pl.pallas_call(functools.partial(kernel, planes), out_shape=jax.ShapeDtyp...]
where the time goes in v4:
time: 75.6 us; the launch traced here: 75.4 us
  Pallas kernels  72 us (95%)
  local copies, waits for them, and re-layouts  3.4 us (4%)
    pallas_call x1, Pallas kernels, on_device(): pl.pallas_call(functools.partial(kernel, planes), out_shape=jax.ShapeDtyp...  72 us
    unnamed x1, local copies, waits for them, and re-layouts  3.4 us

profile of v4, /device:TPU:1, one launch (start us, length us, event | category | flops | bytes accessed | tf_op | source)
XLA Modules:
  0.0 75.4 jit_solution(332790841913794300)
XLA Ops:
  0.0 72.0 %shard_map.46 = f32[512,1280]{1,0:T(8,128)} custom-call(bf16[512,1280]{1,0:T(8,128)(2,1)} %bitcast.5, bf16[1,2]{1,0:T(2,128)(2,1)} %bitcast.7, f32[1,256]{1,0:T(1,128)} %bitcast.6, s32[1,2]{1,0:T(1,128)} %kept_hbm.1), custom_call_target="tpu_custom_call" | custom-call | flops 4026531840 | bytes 3932160 | tf_op jit(solution)/shard_map/pallas_call | solution.py:347
  72.0 3.4 %copy.6 = f32[2,256,1280]{2,1,0:T(8,128)} copy(f32[2,256,1280]{2,1,0:T(8,128)} %bitcast.4) | data formatting | bytes 5242880

commit v5 on v4

--- a/solution.py
+++ b/solution.py
@@ -297,16 +297,12 @@
 
     pieces = ((lo_mine, cut), (lo_mine + cut, rest), (lo_others, cut), (lo_others + cut, rest))
 
-    def apply(slots, piece, earlier):
+    def apply(slots, piece, i, total):
         c = columns_at(*piece)
-        out = []
-        for i in range(2):
-            total = earlier(i)
-            for slot in slots:
-                term = jnp.dot(tt[2 * ORDER.index(slot) + i], bb[slot, :, c], preferred_element_type=F32)
-                total = term if total is None else total + term
-            out.append(total)
-        return out
+        for slot in slots:
+            term = jnp.dot(tt[2 * ORDER.index(slot) + i], bb[slot, :, c], preferred_element_type=F32)
+            total = term if total is None else total + term
+        return total
 
     orient(0)
     second[3].wait_recv()
@@ -314,8 +310,8 @@
     for n, piece in enumerate(pieces):
         if n < 2:
             diagonal[n].wait_recv()
-        for i, total in enumerate(apply((X, D) if n < 2 else (X,), piece, lambda i: None)):
-            g[i * slab:(i + 1) * slab, at:at + piece[1]] = total
+        for i in range(2):
+            g[i * slab:(i + 1) * slab, at:at + piece[1]] = apply((X, D) if n < 2 else (X,), piece, i, None)
         at += piece[1]
     orient(1)
     second[1].wait_recv()
@@ -327,11 +323,12 @@
         if n >= 2:
             diagonal[n].wait_recv()
         slots = (F, R) if n < 2 else (F, R, D)
-        for i, total in enumerate(apply(slots, piece, lambda i: g[i * slab:(i + 1) * slab, here])):
-            g[i * slab:(i + 1) * slab, here] = total
-        result = pltpu.make_async_copy(g.at[:, here], out_hbm.at[:, columns_at(*piece)], out_sem.at[n])
-        result.start()
-        results.append(result)
+        for i in range(2):
+            r = slice(i * slab, (i + 1) * slab)
+            g[r, here] = apply(slots, piece, i, g[r, here])
+            result = pltpu.make_async_copy(g.at[r, here], out_hbm.at[r, columns_at(*piece)], out_sem.at[2 * n + i])
+            result.start()
+            results.append(result)
         at += piece[1]
     for c in started:
         c.wait_send()
@@ -373,7 +370,7 @@
             pltpu.SemaphoreType.DMA((copies,)),
             pltpu.SemaphoreType.DMA((copies,)),
             pltpu.SemaphoreType.DMA((4,)),
-            pltpu.SemaphoreType.DMA((4,)),
+            pltpu.SemaphoreType.DMA((8,)),
         ],
         compiler_params=pltpu.CompilerParams(
             collective_id=0, has_side_effects=True, vmem_limit_bytes=60 * 1024 * 1024

time: 75.6 us -> 75.6 us (level)
  no operation moved by 1% of the time
where the time goes in v5:
time: 75.6 us; the launch traced here: 75.5 us
  Pallas kernels  72 us (95%)
  local copies, waits for them, and re-layouts  3.4 us (4%)
    pallas_call x1, Pallas kernels, on_device(): pl.pallas_call(functools.partial(kernel, planes), out_shape=jax.ShapeDtyp...  72 us
    unnamed x1, local copies, waits for them, and re-layouts  3.4 us

profile of v5, /device:TPU:1, one launch (start us, length us, event | category | flops | bytes accessed | tf_op | source)
XLA Modules:
  0.0 75.5 jit_solution(7826012327747518030)
XLA Ops:
  0.0 72.0 %shard_map.46 = f32[512,1280]{1,0:T(8,128)} custom-call(bf16[512,1280]{1,0:T(8,128)(2,1)} %bitcast.5, bf16[1,2]{1,0:T(2,128)(2,1)} %bitcast.7, f32[1,256]{1,0:T(1,128)} %bitcast.6, s32[1,2]{1,0:T(1,128)} %kept_hbm.1), custom_call_target="tpu_custom_call" | custom-call | flops 4026531840 | bytes 3932160 | tf_op jit(solution)/shard_map/pallas_call | solution.py:344
  72.1 3.4 %copy.6 = f32[2,256,1280]{2,1,0:T(8,128)} copy(f32[2,256,1280]{2,1,0:T(8,128)} %bitcast.4) | data formatting | bytes 5242880
